TPU v7x, 32 devices: a whole 2x2x4 slice. The times are simulated.
32 devices in a mesh: fsdp: 4 (over z), ctx: 4 (over y, core), tp: 2 (over x).
Axes of the slice: x: 2, y: 2, z: 4, core: 2. Of those that a mesh axis runs over, the one named last changes fastest.
Arguments:
- block_input: bfloat16 [4, 1024, 1024], P('fsdp', 'ctx'), may hold values from -6 to 6
- input_gain: float32 [1024], replicated, may hold values from 0.5 to 1.5
- gate_proj: bfloat16 [1024, 2048], P('fsdp', 'tp'), may hold values from -0.1875 to 0.1875
- x_proj: bfloat16 [1024, 2048], P('fsdp', 'tp'), may hold values from -0.1875 to 0.1875
- bc_proj: bfloat16 [1024, 256], P('fsdp'), may hold values from -0.1875 to 0.1875
- dt_proj: bfloat16 [1024, 32], P('fsdp', 'tp'), may hold values from -0.1875 to 0.1875
- x_conv: float32 [4, 2048], P(None, 'tp'), may hold values from -3 to 3
- bc_conv: float32 [4, 256], replicated, may hold values from -3 to 3
- dt_bias: float32 [32], P('tp'), may hold values from -2 to 1
- a_log: float32 [32], P('tp'), may hold values from -11 to -2
- skip_gain: float32 [32], P('tp'), may hold values from 0.5 to 1.5
- gated_gain: float32 [2048], P('tp'), may hold values from 0.5 to 1.5
- out_proj: bfloat16 [2048, 1024], P('tp', 'fsdp'), may hold values from -0.125 to 0.125
- cotangent: bfloat16 [4, 1024, 1024], P('fsdp', 'ctx'), may hold values from -6 to 6
Outputs:
- block_output: bfloat16 [4, 1024, 1024], P('fsdp', 'ctx')
- input_grad: float32 [4, 1024, 1024], P('fsdp', 'ctx')
- grad_input_gain: float32 [1024], replicated
- grad_gate_proj: float32 [1024, 2048], P('fsdp', 'tp')
- grad_x_proj: float32 [1024, 2048], P('fsdp', 'tp')
- grad_bc_proj: float32 [1024, 256], P('fsdp')
- grad_dt_proj: float32 [1024, 32], P('fsdp', 'tp')
- grad_x_conv: float32 [4, 2048], P(None, 'tp')
- grad_bc_conv: float32 [4, 256], replicated
- grad_dt_bias: float32 [32], P('tp')
- grad_a_log: float32 [32], P('tp')
- grad_skip_gain: float32 [32], P('tp')
- grad_gated_gain: float32 [2048], P('tp')
- grad_out_proj: float32 [2048, 1024], P('tp', 'fsdp')
All inputs are finite; a program needn't handle non-finite values.
Results may differ from a plain program's by a relative error of at most 0.0098.
Values may be sent and summed in bfloat16 or wider, within the bound.
No kernel may reach another device: no remote copies, remote signals or barrier semaphores. Data moves between devices by JAX's collectives and lax.ppermute only.
A program may use at most 128 MiB of HBM per device.

v0:
```python
import jax
import jax.numpy as jnp
from jax import lax
from jax.sharding import PartitionSpec as P

EPSILON = 1e-05
FINE = lax.Precision.HIGHEST


def from_behind(block, axis, distance):
    devices = range(lax.axis_size(axis))
    route = [(i - distance, i) for i in devices if i - distance in devices]
    return lax.ppermute(block, axis, route)


def carried_in(part, axis, combine, identity, reverse):
    count = lax.axis_size(axis)
    place = lax.axis_index(axis)
    ahead = count - 1 - place if reverse else place
    gathered = jax.tree.map(lambda a: lax.all_gather(a, axis), part)
    state = jax.tree.map(lambda a, e: jnp.zeros_like(a) + jnp.asarray(e, a.dtype), part, identity)

    def one(lap, state):
        source = count - 1 - lap if reverse else lap
        return combine(
            state, jax.tree.map(lambda a: lax.dynamic_index_in_dim(a, source, 0, False), gathered)
        )

    return lax.fori_loop(0, ahead, one, state)


def combine_states(earlier, later):
    return (earlier[0] * later[0], earlier[1] * later[0][:, :, None, None] + later[1])


def silu_slope(values):
    sigmoid_value = jax.nn.sigmoid(values)
    return sigmoid_value * (1.0 + values * (1.0 - sigmoid_value))


def block_local(x_heads, b_rows, c_rows, step_size, log_decay):
    cumulative = jnp.cumsum(log_decay, axis=2)
    log_gaps = cumulative[:, :, :, None] - cumulative[:, :, None, :]
    length = log_decay.shape[2]
    causal = jnp.tril(jnp.ones((length, length), jnp.bool_))
    decays = jnp.where(causal, jnp.exp(jnp.where(causal, log_gaps, 0.0)), 0.0)
    scores = jnp.einsum("btn,bsn->bts", c_rows, b_rows, precision=FINE)
    weights = decays * scores[:, None, :, :] * step_size[:, :, None, :]
    within = jnp.einsum("bhts,bshp->bthp", weights, x_heads, precision=FINE)
    tail_decay = jnp.exp(cumulative[:, :, -1:] - cumulative) * step_size
    summary = jnp.einsum("bhs,bshp,bsn->bhpn", tail_decay, x_heads, b_rows, precision=FINE)
    return (within, summary, jnp.exp(cumulative[:, :, -1]))


def block_carry(c_rows, log_decay, state_in):
    cumulative = jnp.cumsum(log_decay, axis=2)
    carried = jnp.einsum("btn,bhpn->bthp", c_rows, state_in, precision=FINE)
    return jnp.exp(cumulative).transpose(0, 2, 1)[:, :, :, None] * carried


def back_product(grad_low, weight):
    return lax.dot_general(
        grad_low, weight, (((1,), (1,)), ((), ())), preferred_element_type=jnp.float32
    )


def on_device(
    block_input,
    input_gain,
    gate_proj,
    x_proj,
    bc_proj,
    dt_proj,
    x_conv,
    bc_conv,
    dt_bias,
    a_log,
    skip_gain,
    gated_gain,
    out_proj,
    cotangent,
):
    seqs_here, length, model_width = block_input.shape
    row_count = seqs_here * length
    inner_here = gate_proj.shape[1]
    heads_here = dt_proj.shape[1]
    head_size = inner_here // heads_here
    state_size = bc_proj.shape[1] // 2
    tap_count = x_conv.shape[0]
    full_inner = inner_here * lax.axis_size("tp")
    full_gate, full_x, full_bc, full_dt, full_out = (
        lax.all_gather(gate_proj, "fsdp", axis=0, tiled=True),
        lax.all_gather(x_proj, "fsdp", axis=0, tiled=True),
        lax.all_gather(bc_proj, "fsdp", axis=0, tiled=True),
        lax.all_gather(dt_proj, "fsdp", axis=0, tiled=True),
        lax.all_gather(out_proj, "fsdp", axis=1, tiled=True),
    )
    residual = block_input.astype(jnp.float32)
    in_scale = lax.rsqrt(jnp.mean(residual * residual, axis=-1, keepdims=True) + EPSILON)
    normed_low = (
        (residual * in_scale * input_gain).astype(jnp.bfloat16).reshape(row_count, model_width)
    )
    gate_input = jnp.dot(normed_low, full_gate, preferred_element_type=jnp.float32).reshape(
        seqs_here, length, inner_here
    )
    x_input = jnp.dot(normed_low, full_x, preferred_element_type=jnp.float32).reshape(
        seqs_here, length, inner_here
    )
    bc_input = jnp.dot(normed_low, full_bc, preferred_element_type=jnp.float32).reshape(
        seqs_here, length, 2 * state_size
    )
    dt_input = jnp.dot(normed_low, full_dt, preferred_element_type=jnp.float32).reshape(
        seqs_here, length, heads_here
    )
    conv_input = jnp.concatenate([x_input, bc_input], axis=-1)
    conv_taps = jnp.concatenate([x_conv, bc_conv], axis=-1)
    edge_rows = from_behind(conv_input[:, length - tap_count + 1 :, :], "ctx", 1)
    padded = jnp.concatenate([edge_rows, conv_input], axis=1)
    conv_out = jnp.zeros_like(conv_input)
    for offset in range(tap_count):
        conv_out = conv_out + conv_taps[offset] * padded[:, offset : offset + length, :]
    activated = jax.nn.silu(conv_out)
    x_heads = activated[:, :, :inner_here].reshape(seqs_here, length, heads_here, head_size)
    b_rows = activated[:, :, inner_here : inner_here + state_size]
    c_rows = activated[:, :, inner_here + state_size :]
    pre_step = dt_input.transpose(0, 2, 1) + dt_bias[None, :, None]
    step_size = jax.nn.softplus(pre_step)
    decay_rates = jnp.exp(a_log)[None, :, None]
    log_decay = -decay_rates * step_size
    (within, summary, total_decay), local_back = jax.vjp(
        block_local, x_heads, b_rows, c_rows, step_size, log_decay
    )
    identity = (jnp.ones_like(total_decay), jnp.zeros_like(summary))
    state_in = carried_in((total_decay, summary), "ctx", combine_states, identity, False)[1]
    carried, carry_back = jax.vjp(block_carry, c_rows, log_decay, state_in)
    mixed_heads = within + carried + skip_gain[None, None, :, None] * x_heads
    mixed_flat = mixed_heads.reshape(seqs_here, length, inner_here)
    gate_act = jax.nn.silu(gate_input)
    gated_rows = mixed_flat * gate_act
    square_sum = lax.psum(jnp.sum(gated_rows * gated_rows, axis=-1), "tp")
    out_scale = lax.rsqrt(square_sum / full_inner + EPSILON)[:, :, None]
    normed_out = (
        (gated_rows * out_scale * gated_gain).astype(jnp.bfloat16).reshape(row_count, inner_here)
    )
    branch_sum = lax.psum(jnp.dot(normed_out, full_out, preferred_element_type=jnp.float32), "tp")
    block_output = (residual + branch_sum.reshape(seqs_here, length, model_width)).astype(
        jnp.bfloat16
    )
    cot_rows = cotangent.reshape(row_count, model_width)
    grad_out_w = lax.dot_general(
        normed_out, cot_rows, (((0,), (0,)), ((), ())), preferred_element_type=jnp.float32
    )
    d_normed_low = back_product(cot_rows, full_out).astype(jnp.bfloat16)
    d_normed_out = d_normed_low.astype(jnp.float32).reshape(seqs_here, length, inner_here)
    grad_gated_gain = jnp.sum(d_normed_out * gated_rows * out_scale, axis=(0, 1))
    cross_sum = lax.psum(jnp.sum(d_normed_out * gated_gain * gated_rows, axis=-1), "tp")
    d_gated = (
        out_scale * gated_gain * d_normed_out
        - gated_rows * (out_scale**3 / full_inner) * cross_sum[:, :, None]
    )
    d_mixed = (d_gated * gate_act).reshape(seqs_here, length, heads_here, head_size)
    d_gate_low = (
        (d_gated * mixed_flat * silu_slope(gate_input))
        .astype(jnp.bfloat16)
        .reshape(row_count, inner_here)
    )
    grad_skip_gain = jnp.sum(d_mixed * x_heads, axis=(0, 1, 3))
    d_c_carry, d_decay_carry, state_grad = carry_back(d_mixed)
    later_grad = carried_in((total_decay, state_grad), "ctx", combine_states, identity, True)[1]
    d_total = jnp.sum(later_grad * state_in, axis=(2, 3))
    d_x_heads, d_b_rows, d_c_rows, d_step, d_log_decay = local_back((d_mixed, later_grad, d_total))
    d_x_heads = d_x_heads + skip_gain[None, None, :, None] * d_mixed
    d_c_rows = d_c_rows + d_c_carry
    d_log_decay = d_log_decay + d_decay_carry
    grad_a_log = jnp.sum(d_log_decay * log_decay, axis=(0, 2))
    d_pre = (d_step - decay_rates * d_log_decay) * jax.nn.sigmoid(pre_step)
    grad_dt_bias = jnp.sum(d_pre, axis=(0, 2))
    d_dt_low = d_pre.transpose(0, 2, 1).astype(jnp.bfloat16).reshape(row_count, heads_here)
    d_activated = jnp.concatenate(
        [d_x_heads.reshape(seqs_here, length, inner_here), d_b_rows, d_c_rows], axis=-1
    )
    d_conv_out = d_activated * silu_slope(conv_out)
    d_padded = jnp.zeros_like(padded)
    tap_grads = []
    for offset in range(tap_count):
        tap_grads.append(jnp.sum(d_conv_out * padded[:, offset : offset + length, :], axis=(0, 1)))
        d_padded = d_padded.at[:, offset : offset + length, :].add(conv_taps[offset] * d_conv_out)
    grad_taps = jnp.stack(tap_grads)
    edge_grad = from_behind(d_padded[:, : tap_count - 1, :], "ctx", -1)
    d_conv_input = d_padded[:, tap_count - 1 :, :] + jnp.pad(
        edge_grad, ((0, 0), (length - tap_count + 1, 0), (0, 0))
    )
    d_x_low = d_conv_input[:, :, :inner_here].astype(jnp.bfloat16).reshape(row_count, inner_here)
    partial_normed = (
        back_product(d_gate_low, full_gate)
        + back_product(d_x_low, full_x)
        + back_product(d_dt_low, full_dt)
    )
    summed_normed, summed_bc, grad_bc_conv = lax.psum(
        (
            partial_normed,
            d_conv_input[:, :, inner_here:].reshape(row_count, 2 * state_size),
            grad_taps[:, inner_here:],
        ),
        "tp",
    )
    d_bc_low = summed_bc.astype(jnp.bfloat16)
    d_normed = (summed_normed + back_product(d_bc_low, full_bc)).reshape(
        seqs_here, length, model_width
    )

    def weight_grad(grad_low):
        return lax.dot_general(
            normed_low, grad_low, (((0,), (0,)), ((), ())), preferred_element_type=jnp.float32
        )

    weight_grads = (
        weight_grad(d_gate_low),
        weight_grad(d_x_low),
        weight_grad(d_bc_low),
        weight_grad(d_dt_low),
        grad_out_w,
    )
    grad_input_gain = jnp.sum(d_normed * residual * in_scale, axis=(0, 1))
    d_scaled = d_normed * input_gain
    input_grad = (
        cotangent.astype(jnp.float32)
        + in_scale * d_scaled
        - residual
        * (in_scale**3 / model_width)
        * jnp.sum(d_scaled * residual, axis=-1, keepdims=True)
    )
    sectioned = (
        lax.psum_scatter(weight_grads[0], "fsdp", scatter_dimension=0, tiled=True),
        lax.psum_scatter(weight_grads[1], "fsdp", scatter_dimension=0, tiled=True),
        lax.psum_scatter(weight_grads[2], "fsdp", scatter_dimension=0, tiled=True),
        lax.psum_scatter(weight_grads[3], "fsdp", scatter_dimension=0, tiled=True),
        lax.psum_scatter(weight_grads[4], "fsdp", scatter_dimension=1, tiled=True),
    )
    owned_rows = (
        lax.psum_scatter(sectioned[0], "ctx", scatter_dimension=0, tiled=True),
        lax.psum_scatter(sectioned[1], "ctx", scatter_dimension=0, tiled=True),
        lax.psum_scatter(sectioned[2], "ctx", scatter_dimension=0, tiled=True),
        lax.psum_scatter(sectioned[3], "ctx", scatter_dimension=0, tiled=True),
        lax.psum_scatter(sectioned[4], "ctx", scatter_dimension=1, tiled=True),
    )
    grad_gate_proj, grad_x_proj, grad_bc_proj, grad_dt_proj, grad_out_proj = (
        lax.all_gather(owned_rows[0], "ctx", axis=0, tiled=True),
        lax.all_gather(owned_rows[1], "ctx", axis=0, tiled=True),
        lax.all_gather(owned_rows[2], "ctx", axis=0, tiled=True),
        lax.all_gather(owned_rows[3], "ctx", axis=0, tiled=True),
        lax.all_gather(owned_rows[4], "ctx", axis=1, tiled=True),
    )
    small_totals = lax.psum(
        (
            grad_input_gain,
            grad_taps[:, :inner_here],
            grad_bc_conv,
            grad_dt_bias,
            grad_a_log,
            grad_skip_gain,
            grad_gated_gain,
        ),
        ("fsdp", "ctx"),
    )
    return (
        block_output,
        input_grad,
        small_totals[0],
        grad_gate_proj,
        grad_x_proj,
        grad_bc_proj,
        grad_dt_proj,
        small_totals[1],
        small_totals[2],
        small_totals[3],
        small_totals[4],
        small_totals[5],
        small_totals[6],
        grad_out_proj,
    )


def solution(mesh):
    in_specs = (
        P("fsdp", "ctx", None),
        P(),
        P("fsdp", "tp"),
        P("fsdp", "tp"),
        P("fsdp", None),
        P("fsdp", "tp"),
        P(None, "tp"),
        P(),
        P("tp"),
        P("tp"),
        P("tp"),
        P("tp"),
        P("tp", "fsdp"),
        P("fsdp", "ctx", None),
    )
    out_specs = (
        P("fsdp", "ctx", None),
        P("fsdp", "ctx", None),
        P(),
        P("fsdp", "tp"),
        P("fsdp", "tp"),
        P("fsdp", None),
        P("fsdp", "tp"),
        P(None, "tp"),
        P(),
        P("tp"),
        P("tp"),
        P("tp"),
        P("tp"),
        P("tp", "fsdp"),
    )
    return jax.shard_map(
        on_device, mesh=mesh, in_specs=in_specs, out_specs=out_specs, check_vma=False
    )
```

profile of v0, /device:TPU:0, one launch (start us, length us, event | category | flops | bytes accessed | tf_op | source)
XLA Modules:
  0.0 786.6 jit_solution(12926951627118034505)
XLA Ops:
  8.0 15.0 %all_gather.50 = bf16[1024,16]{0,1:T(8,128)(2,1)S(1)} all-gather(bf16[256,16]{0,1:T(8,128)(2,1)} %param.31), channel_id=1, replica_groups=mesh['fsdp'=4,'ctx'=4,'tp'=2] {'fsdp'}, dimensions={0}, use_global_device_ids=true | all-gather | bytes 40960 | tf_op jit(solution)/shard_map/all_gather | solution.py:95
  29.3 22.7 %all_gather.49 = bf16[1024,256]{1,0:T(8,128)(2,1)S(1)} all-gather(bf16[256,256]{1,0:T(8,128)(2,1)S(1)} %copy-done.44), channel_id=1, replica_groups=mesh['fsdp'=4,'ctx'=4,'tp'=2] {'fsdp'}, dimensions={0}, use_global_device_ids=true | all-gather | bytes 655360 | tf_op jit(solution)/shard_map/all_gather | solution.py:94
  54.0 12.6 %all-gather.13.cloned.1.call-done = bf16[1024,1024]{1,0:T(8,128)(2,1)} async-done(((bf16[256,1024]{1,0:T(8,128)(2,1)}), bf16[1024,1024]{1,0:T(8,128)(2,1)}) %all-gather.13.cloned.1.call-update) | async-done | bytes 2097168 | tf_op jit(solution)/shard_map/all_gather | solution.py:93
  77.2 3.0 fusion.62
  83.0 7.0 all-gather
  91.1 2.6 copy.207
  96.4 7.8 all-gather.25.cloned.1.call-done
  106.3 6.0 fusion.36
  112.3 2.6 copy.205
  114.9 36.8 %all-gather.15.cloned.1.call-done = bf16[1024,1024]{1,0:T(8,128)(2,1)} async-done(((bf16[256,1024]{1,0:T(8,128)(2,1)}), bf16[1024,1024]{1,0:T(8,128)(2,1)}) %all-gather.15.cloned.1.call-update) | async-done | bytes 2097168 | tf_op jit(solution)/shard_map/all_gather | solution.py:92
  151.7 3.7 multiply_reduce_fusion.8
  155.4 4.9 psum.91
  160.3 37.8 %all-gather.17.cloned.1.call-done = bf16[1024,1024]{1,0:T(8,128)(2,1)} async-done(((bf16[1024,256]{1,0:T(8,128)(2,1)}), bf16[1024,1024]{1,0:T(8,128)(2,1)}) %all-gather.17.cloned.1.call-update) | async-done | bytes 2097168 | tf_op jit(solution)/shard_map/all_gather | solution.py:96
  198.2 4.0 fusion.49
  202.2 5.4 psum.93
  207.6 2.9 fusion.59
  212.6 2.6 copy.208
  215.3 3.0 fusion.88
  221.5 2.8 fusion.121
  224.3 3.9 fusion.68
  228.3 2.6 copy.211
  231.0 8.6 %fusion.8 = (f32[16,256]{1,0:T(8,128)}, f32[16,256]{1,0:T(8,128)}, f32[16,256]{1,0:T(8,128)}, f32[256,256]{1,0:T(8,128)S(1)}) fusion(f32[16,256]{1,0:T(8,128)S(1)} %copy-done.57, f32[256,256]{1,0:T(8,128)} %fusion.92, f32[16,256]{1,0:T(8,128)S(1)} %copy-done.59, pred[256,256]{1,0:T(8,128)(4,1)} %iota_compare_fusion, f32[16,64,256]{2,1,0:T(8,128)} %bitcast.308, ...), kind=kOutput, calls=%fused_computation.20 | convolution fusion | flops 820957184 | bytes 2768896 | tf_op jit(solution)/shard_map/transpose(jvp(bhts,bshp->bthp))/dot_general | solution.py:49
  244.2 6.0 while.31
  252.7 4.9 fusion.30
  257.6 2.5 copy.216
  260.2 3.1 fusion.42
  263.3 2.6 multiply_reduce_fusion.5
  268.7 4.5 scatter-add.11
  273.2 2.6 slice_add_fusion.1
  275.8 4.4 scatter-add.14
  286.6 2.8 fusion.77
  300.4 12.9 %all-reduce.11 = (bf16[256,256]{1,0:T(8,128)(2,1)S(1)}, f32[4,256]{1,0:T(4,128)}) all-reduce(f32[256,256]{1,0:T(8,128)S(1)} %slice_bitcast_fusion, f32[4,256]{1,0:T(4,128)S(1)} %pad_maximum_fusion.2), channel_id=1, replica_groups=mesh['fsdp'=4,'ctx'=4,'tp'=2] {'tp'}, use_global_device_ids=true, to_apply=%region_24.25 | all-reduce | flops 66560 | bytes 401408 | tf_op jit(solution)/shard_map/psum | solution.py:199
  314.8 3.4 reduce-scatter.15.cloned.1.call-done
  318.3 79.6 %reduce-scatter.29.cloned.1.call-done = f32[1024,256]{1,0:T(8,128)} async-done(((f32[1024,1024]{1,0:T(8,128)}), f32[1024,256]{1,0:T(8,128)}) %reduce-scatter.29.cloned.1.call-update) | async-done | bytes 1048592 | tf_op jit(solution)/shard_map/reduce_scatter | solution.py:238
  400.6 77.0 %reduce-scatter.19.cloned.1.call-done = f32[256,1024]{1,0:T(8,128)} async-done(((f32[1024,1024]{1,0:T(8,128)}), f32[256,1024]{1,0:T(8,128)}) %reduce-scatter.19.cloned.1.call-update) | async-done | bytes 1048592 | tf_op jit(solution)/shard_map/reduce_scatter | solution.py:235
  477.6 3.5 convolution_bitcast_fusion
  483.5 16.5 %reduce-scatter.27.cloned.1.call-done = f32[256,16]{0,1:T(8,128)} async-done(((f32[1024,16]{0,1:T(8,128)}), f32[256,16]{0,1:T(8,128)}) %reduce-scatter.27.cloned.1.call-update) | async-done | bytes 16400 | tf_op jit(solution)/shard_map/reduce_scatter | solution.py:237
  502.9 25.2 %reduce-scatter.23.cloned.1.call-done = f32[256,256]{1,0:T(8,128)} async-done(((f32[1024,256]{1,0:T(8,128)}), f32[256,256]{1,0:T(8,128)}) %reduce-scatter.23.cloned.1.call-update) | async-done | bytes 262160 | tf_op jit(solution)/shard_map/reduce_scatter | solution.py:236
  528.2 26.2 %reduce-scatter.17.cloned.1.call-done = f32[64,1024]{1,0:T(8,128)} async-done(((f32[256,1024]{1,0:T(8,128)}), f32[64,1024]{1,0:T(8,128)}) %reduce-scatter.17.cloned.1.call-update) | async-done | bytes 262160 | tf_op jit(solution)/shard_map/reduce_scatter | solution.py:241
  554.4 27.2 %reduce-scatter.33.cloned.1.call-done = f32[64,1024]{1,0:T(8,128)} async-done(((f32[256,1024]{1,0:T(8,128)}), f32[64,1024]{1,0:T(8,128)}) %reduce-scatter.33.cloned.1.call-update) | async-done | bytes 262160
  581.7 27.6 %reduce-scatter.21.cloned.1.call-done = f32[64,1024]{1,0:T(8,128)} async-done(((f32[256,1024]{1,0:T(8,128)}), f32[64,1024]{1,0:T(8,128)}) %reduce-scatter.21.cloned.1.call-update) | async-done | bytes 262160 | tf_op jit(solution)/shard_map/reduce_scatter | solution.py:242
  609.5 22.1 %reduce-scatter.31.cloned.1.call-done = f32[64,16]{1,0:T(8,128)} async-done(((f32[256,16]{1,0:T(8,128)}), f32[64,16]{1,0:T(8,128)}) %reduce-scatter.31.cloned.1.call-update) | async-done | bytes 4112
  632.5 5.2 all-gather.3
  638.4 59.9 %all-reduce.10.cloned.1.call-done = (f32[1,256,1024]{2,1,0:T(8,128)}, f32[256,1024]{1,0:T(8,128)}) async-done(((f32[1,256,1024]{2,1,0:T(8,128)}, f32[256,1024]{1,0:T(8,128)}), (f32[1,256,1024]{2,1,0:T(8,128)}, f32[256,1024]{1,0:T(8,128)})) %all-reduce.10.cloned.1.call-update) | async-done | bytes 2097168 | tf_op jit(solution)/shard_map/psum | solution.py:145
  700.2 62.2 %all-reduce.4 = (f32[1024]{0:T(1024)}, f32[4,1024]{1,0:T(4,128)}, f32[4,256]{1,0:T(4,128)}, f32[16]{0:T(128)}, f32[16]{0:T(128)}, /*index=5*/f32[16]{0:T(128)}, f32[1024]{0:T(1024)}) all-reduce(f32[1024]{0:T(1024)S(1)} %get-tuple-element.317, f32[4,1024]{1,0:T(4,128)S(1)} %slice.219, ...), channel_id=1, replica_groups=mesh['fsdp'=4,'ctx'=4,'tp'=2] {'fsdp','ctx'}, use_global_device_ids=true, to_apply=%region_27.28 | all-reduce | flops 7216 | bytes 57728 | tf_op jit(solution)/shard_map/psum | solution.py:254
  762.5 2.8 fusion.55
  765.2 7.0 all_gather.60
  772.3 2.6 copy.228
  (303 shorter events, 84.4 us)
Async XLA Ops:
  7.2 59.4 %all-gather.13.cloned.1.call-start = ((), (), s32[]{:S(2)}) async-start(), calls=%async_computation.10 | async-start | bytes 2621440 | tf_op jit(solution)/shard_map/all_gather | solution.py:93
  7.9 96.3 %all-gather.25.cloned.1.call-start = ((), (), s32[]{:S(2)}) async-start(), calls=%async_computation.24 | async-start | bytes 2621440 | tf_op jit(solution)/shard_map/all_gather | solution.py:20
  23.0 6.3 copy-start.44
  26.0 26.7 %copy-start.2 = (bf16[1,256,1024]{2,1,0:T(8,128)(2,1)S(1)}, bf16[1,256,1024]{2,1,0:T(8,128)(2,1)}, u32[]{:S(2)}) copy-start(bf16[1,256,1024]{2,1,0:T(8,128)(2,1)} %param.26) | copy-start | bytes 1572868
  26.1 26.7 %copy-start.37 = (f32[1024]{0:T(1024)S(1)}, f32[1024]{0:T(1024)}, u32[]{:S(2)}) copy-start(f32[1024]{0:T(1024)} %param.27) | copy-start | bytes 12292
  27.6 25.6 %copy-start.33 = (f32[1,16,256]{1,2,0:T(8,128)}, f32[1,16,256]{1,2,0:T(8,128)S(1)}, u32[]{:S(2)}) copy-start(f32[1,16,256]{1,2,0:T(8,128)S(1)} %get-tuple-element.380) | copy-start | bytes 49156
  27.6 25.6 %copy-start.29 = (f32[1,16,256]{1,2,0:T(8,128)}, f32[1,16,256]{1,2,0:T(8,128)S(1)}, u32[]{:S(2)}) copy-start(f32[1,16,256]{1,2,0:T(8,128)S(1)} %get-tuple-element.381) | copy-start | bytes 49156
  29.2 24.0 %copy-start.24 = (f32[1,16,256]{1,2,0:T(8,128)}, f32[1,16,256]{1,2,0:T(8,128)S(1)}, u32[]{:S(2)}) copy-start(f32[1,16,256]{1,2,0:T(8,128)S(1)} %get-tuple-element.365) | copy-start | bytes 49156
  53.2 18.5 %copy-start.21 = (f32[1,256,256]{2,1,0:T(8,128)}, f32[1,256,256]{2,1,0:T(8,128)S(1)}, u32[]{:S(2)}) copy-start(f32[1,256,256]{2,1,0:T(8,128)S(1)} %convolution_bitcast_fusion.3) | copy-start | bytes 786436
  53.2 15.7 %copy-start.65 = (f32[16]{0:T(128)}, f32[16]{0:T(128)S(1)}, u32[]{:S(2)}) copy-start(f32[16]{0:T(128)S(1)} %get-tuple-element.374) | copy-start | bytes 196
  69.0 2.6 collective-permute-start
  77.2 29.0 %copy-start.7 = (f32[1,256,1024]{1,2,0:T(8,128)}, f32[1,256,1024]{1,2,0:T(8,128)S(1)}, u32[]{:S(2)}) copy-start(f32[1,256,1024]{1,2,0:T(8,128)S(1)} %copy.193) | copy-start | bytes 3145732
  80.2 9.8 %copy-start.35 = (f32[256,16]{1,0:T(8,128)S(1)}, f32[256,16]{1,0:T(8,128)}, u32[]{:S(2)}) copy-start(f32[256,16]{1,0:T(8,128)} %get-tuple-element.364) | copy-start | bytes 49156
  80.2 71.5 %all-gather.15.cloned.1.call-start = ((), (), s32[]{:S(2)}) async-start(), calls=%async_computation.11 | async-start | bytes 2621440 | tf_op jit(solution)/shard_map/all_gather | solution.py:92
  80.9 117.2 %all-gather.17.cloned.1.call-start = ((), (), s32[]{:S(2)}) async-start(), calls=%async_computation.12 | async-start | bytes 2621440 | tf_op jit(solution)/shard_map/all_gather | solution.py:96
  81.5 162.7 %all-gather.27.cloned.1.call-start = ((), (), s32[]{:S(2)}) async-start(), calls=%async_computation.25 | async-start | bytes 2621440 | tf_op jit(solution)/shard_map/all_gather | solution.py:20
  104.2 8.1 %copy-start.73 = (f32[4,1,16]{2,1,0:T(1,128)}, f32[4,1,16]{2,1,0:T(1,128)S(1)}, u32[]{:S(2)}) copy-start(f32[4,1,16]{2,1,0:T(1,128)S(1)} %get-tuple-element.621) | copy-start | bytes 772
  114.9 83.2 %copy-start.45 = (f32[1024]{0:T(1024)S(1)}, f32[1024]{0:T(1024)}, u32[]{:S(2)}) copy-start(f32[1024]{0:T(1024)} %param.37) | copy-start | bytes 12292
  155.4 69.0 %copy-start.5 = (f32[256,1024]{1,0:T(8,128)}, f32[256,1024]{1,0:T(8,128)S(1)}, u32[]{:S(2)}) copy-start(f32[256,1024]{1,0:T(8,128)S(1)} %get-tuple-element.363) | copy-start | bytes 3145732
  218.3 99.9 %reduce-scatter.15.cloned.1.call-start = ((), (), s32[]{:S(2)}) async-start(), calls=%async_computation.13 | async-start | bytes 5242880 | tf_op jit(solution)/shard_map/reduce_scatter | solution.py:234
  224.3 173.7 %reduce-scatter.29.cloned.1.call-start = ((), (), s32[]{:S(2)}) async-start(), calls=%async_computation.22 | async-start | bytes 5242880 | tf_op jit(solution)/shard_map/reduce_scatter | solution.py:238
  228.3 249.2 %reduce-scatter.19.cloned.1.call-start = ((), (), s32[]{:S(2)}) async-start(), calls=%async_computation.16 | async-start | bytes 5242880 | tf_op jit(solution)/shard_map/reduce_scatter | solution.py:235
  231.0 10.1 %copy-start.13 = (f32[256,1024]{0,1:T(8,128)S(1)}, f32[256,1024]{0,1:T(8,128)}, u32[]{:S(2)}) copy-start(f32[256,1024]{0,1:T(8,128)} %copy.208) | copy-start | bytes 3145732
  280.9 3.1 collective-permute-start.1
  289.5 210.4 %reduce-scatter.27.cloned.1.call-start = ((), (), s32[]{:S(2)}) async-start(), calls=%async_computation.21 | async-start | bytes 81920 | tf_op jit(solution)/shard_map/reduce_scatter | solution.py:237
  293.1 7.2 copy-start.11
  299.3 15.4 %copy-start.40 = (bf16[1,16,256]{1,2,0:T(8,128)(2,1)}, bf16[1,16,256]{1,2,0:T(8,128)(2,1)S(1)}, u32[]{:S(2)}) copy-start(bf16[1,16,256]{1,2,0:T(8,128)(2,1)S(1)} %get-tuple-element.358) | copy-start | bytes 24580
  300.3 227.8 %reduce-scatter.23.cloned.1.call-start = ((), (), s32[]{:S(2)}) async-start(), calls=%async_computation.19 | async-start | bytes 1310720 | tf_op jit(solution)/shard_map/reduce_scatter | solution.py:236
  314.8 239.6 %reduce-scatter.17.cloned.1.call-start = ((), (), s32[]{:S(2)}) async-start(), calls=%async_computation.14 | async-start | bytes 1310720 | tf_op jit(solution)/shard_map/reduce_scatter | solution.py:241
  318.3 263.3 %reduce-scatter.33.cloned.1.call-start = ((), (), s32[]{:S(2)}) async-start(), calls=%async_computation.27 | async-start | bytes 1310720
  400.5 77.1 %copy-start.6 = (f32[256,1024]{1,0:T(8,128)S(1)}, f32[256,1024]{1,0:T(8,128)}, u32[]{:S(2)}) copy-start(f32[256,1024]{1,0:T(8,128)} %copy-done.5) | copy-start | bytes 3145732
  400.5 208.7 %reduce-scatter.21.cloned.1.call-start = ((), (), s32[]{:S(2)}) async-start(), calls=%async_computation.17 | async-start | bytes 1310720 | tf_op jit(solution)/shard_map/reduce_scatter | solution.py:242
  477.5 154.1 %reduce-scatter.31.cloned.1.call-start = ((), (), s32[]{:S(2)}) async-start(), calls=%async_computation.26 | async-start | bytes 163840
  482.7 18.8 %copy-start.41 = (bf16[1,16,256]{1,2,0:T(8,128)(2,1)S(1)}, bf16[1,16,256]{1,2,0:T(8,128)(2,1)}, u32[]{:S(2)}) copy-start(bf16[1,16,256]{1,2,0:T(8,128)(2,1)} %copy-done.40) | copy-start | bytes 24580
  482.7 18.8 %copy-start.43 = (bf16[1024,16]{0,1:T(8,128)(2,1)S(1)}, bf16[1024,16]{0,1:T(8,128)(2,1)}, u32[]{:S(2)}) copy-start(bf16[1024,16]{0,1:T(8,128)(2,1)} %copy-done.42) | copy-start | bytes 98308
  501.5 196.8 %all-reduce.10.cloned.1.call-start = ((), (), s32[]{:S(2)}) async-start(), calls=%async_computation.28 | async-start | bytes 4194304 | tf_op jit(solution)/shard_map/psum | solution.py:145
  502.8 106.5 %copy-start.56 = (f32[1024]{0:T(1024)S(1)}, f32[1024]{0:T(1024)}, u32[]{:S(2)}) copy-start(f32[1024]{0:T(1024)} %get-tuple-element.355) | copy-start | bytes 12292
  502.8 106.7 %copy-start.49 = (f32[1,1280]{1,0:T(1,128)S(1)}, f32[1,1280]{1,0:T(1,128)}, u32[]{:S(2)}) copy-start(f32[1,1280]{1,0:T(1,128)} %copy-done.48) | copy-start | bytes 15364
  502.8 106.7 %copy-start.51 = (f32[1,1280]{1,0:T(1,128)S(1)}, f32[1,1280]{1,0:T(1,128)}, u32[]{:S(2)}) copy-start(f32[1,1280]{1,0:T(1,128)} %copy-done.50) | copy-start | bytes 15364
  502.8 106.7 %copy-start.53 = (f32[1,1280]{1,0:T(1,128)S(1)}, f32[1,1280]{1,0:T(1,128)}, u32[]{:S(2)}) copy-start(f32[1,1280]{1,0:T(1,128)} %copy-done.52) | copy-start | bytes 15364
  502.8 106.7 %copy-start.55 = (f32[1,1280]{1,0:T(1,128)S(1)}, f32[1,1280]{1,0:T(1,128)}, u32[]{:S(2)}) copy-start(f32[1,1280]{1,0:T(1,128)} %copy-done.54) | copy-start | bytes 15364
  502.8 195.5 %copy-start.27 = (bf16[1024,256]{1,0:T(8,128)(2,1)S(1)}, bf16[1024,256]{1,0:T(8,128)(2,1)}, u32[]{:S(2)}) copy-start(bf16[1024,256]{1,0:T(8,128)(2,1)} %copy-done.26) | copy-start | bytes 1572868
  502.8 262.4 %reduce-scatter.25.cloned.1.call-start = ((), (), s32[]{:S(2)}) async-start(), calls=%async_computation.20 | async-start | bytes 327680 | tf_op jit(solution)/shard_map/reduce_scatter | solution.py:243
  528.1 244.2 %all-gather.19.cloned.1.call-start = ((), (), s32[]{:S(2)}) async-start(), calls=%async_computation.15 | async-start | bytes 1310720 | tf_op jit(solution)/shard_map/all_gather | solution.py:248
  554.4 217.9 %all-gather.23.cloned.1.call-start = ((), (), s32[]{:S(2)}) async-start(), calls=%async_computation.23 | async-start | bytes 1310720 | tf_op jit(solution)/shard_map/all_gather | solution.py:252
  581.6 194.9 %all-gather.21.cloned.1.call-start = ((), (), s32[]{:S(2)}) async-start(), calls=%async_computation.18 | async-start | bytes 1310720 | tf_op jit(solution)/shard_map/all_gather | solution.py:249
  698.3 64.1 %copy-start.28 = (bf16[1,256,1024]{2,1,0:T(8,128)(2,1)S(1)}, bf16[1,256,1024]{2,1,0:T(8,128)(2,1)}, u32[]{:S(2)}) copy-start(bf16[1,256,1024]{2,1,0:T(8,128)(2,1)} %param.39) | copy-start | bytes 1572868
  698.3 64.1 %copy-start.70 = (f32[256]{0:T(256)S(1)}, f32[256]{0:T(256)}, u32[]{:S(2)}) copy-start(f32[256]{0:T(256)} %get-tuple-element.376) | copy-start | bytes 3076
  (50 other events, 141.1 us)
Sparse Core Ops, SparseCore 0:
  9.6 56.9 all-gather.12
  80.3 23.7 all-gather.24
  105.7 45.9 all-gather.14
  153.1 44.9 all-gather.16
  218.4 20.8 all-gather.26
  241.5 76.7 reduce-scatter.14
  320.6 77.2 reduce-scatter.28
  400.2 77.2 reduce-scatter.18
  480.4 19.4 reduce-scatter.26
  502.7 25.3 reduce-scatter.22
  530.8 23.5 reduce-scatter.16
  556.7 24.8 reduce-scatter.32
  584.3 24.8 reduce-scatter.20
  612.1 19.5 reduce-scatter.30
  635.2 63.0 all-reduce.9
  700.6 20.0 reduce-scatter.24
  722.2 16.9 all-gather.18
  740.6 16.7 all-gather.22
  759.1 17.4 all-gather.20
where the time goes:
time: 796 us; the launch traced here: 787 us
  waiting for transfers between devices  466 us (59%)
  blocking collectives  142 us (18%)
  matrix products  71.4 us (9%)
  local copies, waits for them, and re-layouts  50.8 us (6%)
  other arithmetic  36.6 us (5%)
  between operations  15.3 us (2%)
    reduce_scatter x1, waiting for transfers between devices, on_device(): lax.psum_scatter(weight_grads[4], 'fsdp', scatter_dimension=1, tiled=True)  79.6 us
    reduce_scatter x1, waiting for transfers between devices, on_device(): lax.psum_scatter(weight_grads[1], 'fsdp', scatter_dimension=0, tiled=True)  77 us
    psum x1, blocking collectives, on_device(): lax.psum((grad_input_gain, grad_taps[:, :inner_here], grad_bc_conv, grad_...  62.2 us
    psum x1, waiting for transfers between devices, on_device(): lax.psum(jnp.dot(normed_out, full_out, preferred_element_type=jnp.float32...  59.9 us
    unnamed x21, waiting for transfers between devices  51.5 us
    all_gather x1, waiting for transfers between devices, on_device(): lax.all_gather(out_proj, 'fsdp', axis=1, tiled=True)  37.8 us
    all_gather x1, waiting for transfers between devices, on_device(): lax.all_gather(gate_proj, 'fsdp', axis=0, tiled=True)  36.8 us
    reduce_scatter x1, waiting for transfers between devices, on_device(): lax.psum_scatter(sectioned[1], 'ctx', scatter_dimension=0, tiled=True)  27.6 us
  transfers between devices with their start and end apart: 21, of which 17 were waited for; matrix products, arithmetic and copies ran while one was open for 16% of the time, Pallas kernels for 0%

commit v1 on v0

--- a/solution.py
+++ b/solution.py
@@ -2,6 +2,7 @@
 import jax.numpy as jnp
 from jax import lax
 from jax.sharding import PartitionSpec as P
+from jax.lax import psum
 
 EPSILON = 1e-05
 FINE = lax.Precision.HIGHEST
@@ -251,18 +252,17 @@
         lax.all_gather(owned_rows[3], "ctx", axis=0, tiled=True),
         lax.all_gather(owned_rows[4], "ctx", axis=1, tiled=True),
     )
-    small_totals = lax.psum(
-        (
-            grad_input_gain,
-            grad_taps[:, :inner_here],
-            grad_bc_conv,
-            grad_dt_bias,
-            grad_a_log,
-            grad_skip_gain,
-            grad_gated_gain,
-        ),
-        ("fsdp", "ctx"),
-    )
+    small_totals = (
+        grad_input_gain,
+        grad_taps[:, :inner_here],
+        grad_bc_conv,
+        grad_dt_bias,
+        grad_a_log,
+        grad_skip_gain,
+        grad_gated_gain,
+    )
+    for p in ("ctx", "fsdp"):
+        small_totals = psum(small_totals, p)
     return (
         block_output,
         input_grad,

time: 796 us -> 797 us (level)
  waiting for transfers between devices: 466 us -> 499 us
  blocking collectives: 142 us -> 110 us
    psum x1 -> x2, blocking collectives: 62.2 us -> 31 us  [on_device(): small_totals = psum(small_totals, p)]
    all_gather x1, waiting for transfers between devices: 0.01 us -> 18.5 us  [on_device(): lax.all_gather(owned_rows[4], 'ctx', axis=1, tiled=True)]
    all_gather x1, waiting for transfers between devices: 1.64 us -> 15.9 us  [on_device(): lax.all_gather(owned_rows[1], 'ctx', axis=0, tiled=True)]
  transfers between devices with their start and end apart: 21 -> 21, of which waited for: 17 -> 18; matrix products, arithmetic and copies ran while one was open for 16% -> 16% of each run, Pallas kernels for 0% -> 0%
where the time goes in v1:
time: 797 us; the launch traced here: 787 us
  waiting for transfers between devices  499 us (63%)
  blocking collectives  110 us (14%)
  matrix products  71.4 us (9%)
  local copies, waits for them, and re-layouts  50.7 us (6%)
  other arithmetic  36.6 us (5%)
  between operations  15.3 us (2%)
    reduce_scatter x1, waiting for transfers between devices, on_device(): lax.psum_scatter(weight_grads[4], 'fsdp', scatter_dimension=1, tiled=True)  79.6 us
    reduce_scatter x1, waiting for transfers between devices, on_device(): lax.psum_scatter(weight_grads[1], 'fsdp', scatter_dimension=0, tiled=True)  77 us
    psum x1, waiting for transfers between devices, on_device(): lax.psum(jnp.dot(normed_out, full_out, preferred_element_type=jnp.float32...  59.9 us
    unnamed x21, waiting for transfers between devices  51.5 us
    all_gather x1, waiting for transfers between devices, on_device(): lax.all_gather(out_proj, 'fsdp', axis=1, tiled=True)  37.9 us
    all_gather x1, waiting for transfers between devices, on_device(): lax.all_gather(gate_proj, 'fsdp', axis=0, tiled=True)  36.8 us
    psum x2, blocking collectives, on_device(): small_totals = psum(small_totals, p)  31 us
    reduce_scatter x1, waiting for transfers between devices, on_device(): lax.psum_scatter(sectioned[1], 'ctx', scatter_dimension=0, tiled=True)  27.6 us
  transfers between devices with their start and end apart: 21, of which 18 were waited for; matrix products, arithmetic and copies ran while one was open for 16% of the time, Pallas kernels for 0%

profile of v1, /device:TPU:0, one launch (start us, length us, event | category | flops | bytes accessed | tf_op | source)
XLA Modules:
  0.0 787.1 jit_solution(7739521720062136200)
XLA Ops:
  8.0 15.0 %all_gather.50 = bf16[1024,16]{0,1:T(8,128)(2,1)S(1)} all-gather(bf16[256,16]{0,1:T(8,128)(2,1)} %param.31), channel_id=1, replica_groups=mesh['fsdp'=4,'ctx'=4,'tp'=2] {'fsdp'}, dimensions={0}, use_global_device_ids=true | all-gather | bytes 40960 | tf_op jit(solution)/shard_map/all_gather | solution.py:96
  29.2 22.7 %all_gather.49 = bf16[1024,256]{1,0:T(8,128)(2,1)S(1)} all-gather(bf16[256,256]{1,0:T(8,128)(2,1)S(1)} %copy-done.44), channel_id=1, replica_groups=mesh['fsdp'=4,'ctx'=4,'tp'=2] {'fsdp'}, dimensions={0}, use_global_device_ids=true | all-gather | bytes 655360 | tf_op jit(solution)/shard_map/all_gather | solution.py:95
  54.0 12.6 %all-gather.13.cloned.1.call-done = bf16[1024,1024]{1,0:T(8,128)(2,1)} async-done(((bf16[256,1024]{1,0:T(8,128)(2,1)}), bf16[1024,1024]{1,0:T(8,128)(2,1)}) %all-gather.13.cloned.1.call-update) | async-done | bytes 2097168 | tf_op jit(solution)/shard_map/all_gather | solution.py:94
  77.2 2.9 fusion.62
  83.0 7.0 all-gather
  91.1 2.6 copy.207
  96.4 7.8 all-gather.25.cloned.1.call-done
  106.3 6.0 fusion.36
  112.3 2.6 copy.205
  114.9 36.8 %all-gather.15.cloned.1.call-done = bf16[1024,1024]{1,0:T(8,128)(2,1)} async-done(((bf16[256,1024]{1,0:T(8,128)(2,1)}), bf16[1024,1024]{1,0:T(8,128)(2,1)}) %all-gather.15.cloned.1.call-update) | async-done | bytes 2097168 | tf_op jit(solution)/shard_map/all_gather | solution.py:93
  151.7 3.7 multiply_reduce_fusion.8
  155.4 4.9 psum.140
  160.3 37.9 %all-gather.17.cloned.1.call-done = bf16[1024,1024]{1,0:T(8,128)(2,1)} async-done(((bf16[1024,256]{1,0:T(8,128)(2,1)}), bf16[1024,1024]{1,0:T(8,128)(2,1)}) %all-gather.17.cloned.1.call-update) | async-done | bytes 2097168 | tf_op jit(solution)/shard_map/all_gather | solution.py:97
  198.2 4.0 fusion.49
  202.2 5.4 psum.142
  207.6 2.9 fusion.59
  212.7 2.6 copy.208
  215.3 3.0 fusion.88
  221.5 2.8 fusion.121
  224.4 3.9 fusion.68
  228.4 2.6 copy.211
  231.0 8.6 %fusion.8 = (f32[16,256]{1,0:T(8,128)}, f32[16,256]{1,0:T(8,128)}, f32[16,256]{1,0:T(8,128)}, f32[256,256]{1,0:T(8,128)S(1)}) fusion(f32[16,256]{1,0:T(8,128)S(1)} %copy-done.57, f32[256,256]{1,0:T(8,128)} %fusion.92, f32[16,256]{1,0:T(8,128)S(1)} %copy-done.59, pred[256,256]{1,0:T(8,128)(4,1)} %iota_compare_fusion, f32[16,64,256]{2,1,0:T(8,128)} %bitcast.308, ...), kind=kOutput, calls=%fused_computation.20 | convolution fusion | flops 820957184 | bytes 2768896 | tf_op jit(solution)/shard_map/transpose(jvp(bhts,bshp->bthp))/dot_general | solution.py:50
  244.3 6.0 while.31
  252.8 4.9 fusion.30
  260.2 3.1 fusion.42
  263.4 2.6 multiply_reduce_fusion.5
  268.7 4.5 scatter-add.11
  275.8 4.4 scatter-add.14
  286.6 2.8 fusion.77
  300.4 12.9 %all-reduce.12 = (bf16[256,256]{1,0:T(8,128)(2,1)S(1)}, f32[4,256]{1,0:T(4,128)}) all-reduce(f32[256,256]{1,0:T(8,128)S(1)} %slice_bitcast_fusion, f32[4,256]{1,0:T(4,128)S(1)} %pad_maximum_fusion.2), channel_id=1, replica_groups=mesh['fsdp'=4,'ctx'=4,'tp'=2] {'tp'}, use_global_device_ids=true, to_apply=%region_24.25 | all-reduce | flops 66560 | bytes 401408 | tf_op jit(solution)/shard_map/psum | solution.py:200
  314.8 3.4 reduce-scatter.15.cloned.1.call-done
  318.4 79.6 %reduce-scatter.29.cloned.1.call-done = f32[1024,256]{1,0:T(8,128)} async-done(((f32[1024,1024]{1,0:T(8,128)}), f32[1024,256]{1,0:T(8,128)}) %reduce-scatter.29.cloned.1.call-update) | async-done | bytes 1048592 | tf_op jit(solution)/shard_map/reduce_scatter | solution.py:239
  400.6 77.0 %reduce-scatter.19.cloned.1.call-done = f32[256,1024]{1,0:T(8,128)} async-done(((f32[1024,1024]{1,0:T(8,128)}), f32[256,1024]{1,0:T(8,128)}) %reduce-scatter.19.cloned.1.call-update) | async-done | bytes 1048592 | tf_op jit(solution)/shard_map/reduce_scatter | solution.py:236
  477.7 3.5 convolution_bitcast_fusion
  483.5 16.5 %reduce-scatter.27.cloned.1.call-done = f32[256,16]{0,1:T(8,128)} async-done(((f32[1024,16]{0,1:T(8,128)}), f32[256,16]{0,1:T(8,128)}) %reduce-scatter.27.cloned.1.call-update) | async-done | bytes 16400 | tf_op jit(solution)/shard_map/reduce_scatter | solution.py:238
  502.9 25.2 %reduce-scatter.23.cloned.1.call-done = f32[256,256]{1,0:T(8,128)} async-done(((f32[1024,256]{1,0:T(8,128)}), f32[256,256]{1,0:T(8,128)}) %reduce-scatter.23.cloned.1.call-update) | async-done | bytes 262160 | tf_op jit(solution)/shard_map/reduce_scatter | solution.py:237
  528.2 26.2 %reduce-scatter.17.cloned.1.call-done = f32[64,1024]{1,0:T(8,128)} async-done(((f32[256,1024]{1,0:T(8,128)}), f32[64,1024]{1,0:T(8,128)}) %reduce-scatter.17.cloned.1.call-update) | async-done | bytes 262160 | tf_op jit(solution)/shard_map/reduce_scatter | solution.py:242
  554.5 27.2 %reduce-scatter.33.cloned.1.call-done = f32[64,1024]{1,0:T(8,128)} async-done(((f32[256,1024]{1,0:T(8,128)}), f32[64,1024]{1,0:T(8,128)}) %reduce-scatter.33.cloned.1.call-update) | async-done | bytes 262160
  581.8 27.6 %reduce-scatter.21.cloned.1.call-done = f32[64,1024]{1,0:T(8,128)} async-done(((f32[256,1024]{1,0:T(8,128)}), f32[64,1024]{1,0:T(8,128)}) %reduce-scatter.21.cloned.1.call-update) | async-done | bytes 262160 | tf_op jit(solution)/shard_map/reduce_scatter | solution.py:243
  609.6 22.1 %reduce-scatter.31.cloned.1.call-done = f32[64,16]{1,0:T(8,128)} async-done(((f32[256,16]{1,0:T(8,128)}), f32[64,16]{1,0:T(8,128)}) %reduce-scatter.31.cloned.1.call-update) | async-done | bytes 4112
  632.6 5.2 all-gather.3
  638.5 59.9 %all-reduce.11.cloned.1.call-done = (f32[1,256,1024]{2,1,0:T(8,128)}, f32[256,1024]{1,0:T(8,128)}) async-done(((f32[1,256,1024]{2,1,0:T(8,128)}, f32[256,1024]{1,0:T(8,128)}), (f32[1,256,1024]{2,1,0:T(8,128)}, f32[256,1024]{1,0:T(8,128)})) %all-reduce.11.cloned.1.call-update) | async-done | bytes 2097168 | tf_op jit(solution)/shard_map/psum | solution.py:146
  700.3 11.4 %all-reduce.4 = (f32[1024]{0:T(1024)S(1)}, f32[4,1024]{1,0:T(4,128)S(1)}, f32[4,256]{1,0:T(4,128)S(1)}, f32[16]{0:T(128)S(1)}, f32[16]{0:T(128)S(1)}, /*index=5*/f32[16]{0:T(128)S(1)}, f32[1024]{0:T(1024)S(1)}) all-reduce(f32[1024]{0:T(1024)S(1)} %get-tuple-element.317, ...), channel_id=1, replica_groups=mesh['fsdp'=4,'ctx'=4,'tp'=2] {'ctx'}, use_global_device_ids=true, to_apply=%region_27.28 | all-reduce | flops 7216 | bytes 57728 | tf_op jit(solution)/shard_map/psum | solution.py:265
  711.8 19.6 %all-reduce.5 = (f32[1024]{0:T(1024)}, f32[4,1024]{1,0:T(4,128)}, f32[4,256]{1,0:T(4,128)}, f32[16]{0:T(128)}, f32[16]{0:T(128)}, /*index=5*/f32[16]{0:T(128)}, f32[1024]{0:T(1024)}) all-reduce(f32[1024]{0:T(1024)S(1)} %get-tuple-element.344, ...), channel_id=1, replica_groups=mesh['fsdp'=4,'ctx'=4,'tp'=2] {'fsdp'}, use_global_device_ids=true, to_apply=%region_28.29 | all-reduce | flops 7216 | bytes 57728 | tf_op jit(solution)/shard_map/psum | solution.py:265
  731.4 2.8 fusion.55
  734.1 6.0 all_gather.60
  740.1 18.5 %all-gather.23.cloned.1.call-done = f32[1024,256]{0,1:T(8,128)} async-done(((f32[1024,64]{0,1:T(8,128)}), f32[1024,256]{0,1:T(8,128)}) %all-gather.23.cloned.1.call-update) | async-done | bytes 1048592 | tf_op jit(solution)/shard_map/all_gather | solution.py:253
  761.2 15.9 %all-gather.21.cloned.1.call-done = f32[256,1024]{1,0:T(8,128)} async-done(((f32[64,1024]{1,0:T(8,128)}), f32[256,1024]{1,0:T(8,128)}) %all-gather.21.cloned.1.call-update) | async-done | bytes 1048592 | tf_op jit(solution)/shard_map/all_gather | solution.py:250
  (304 shorter events, 90.4 us)
Async XLA Ops:
  7.2 59.4 %all-gather.13.cloned.1.call-start = ((), (), s32[]{:S(2)}) async-start(), calls=%async_computation.10 | async-start | bytes 2621440 | tf_op jit(solution)/shard_map/all_gather | solution.py:94
  7.9 96.3 %all-gather.25.cloned.1.call-start = ((), (), s32[]{:S(2)}) async-start(), calls=%async_computation.24 | async-start | bytes 2621440 | tf_op jit(solution)/shard_map/all_gather | solution.py:21
  26.0 26.7 %copy-start.2 = (bf16[1,256,1024]{2,1,0:T(8,128)(2,1)S(1)}, bf16[1,256,1024]{2,1,0:T(8,128)(2,1)}, u32[]{:S(2)}) copy-start(bf16[1,256,1024]{2,1,0:T(8,128)(2,1)} %param.26) | copy-start | bytes 1572868
  26.0 26.7 %copy-start.37 = (f32[1024]{0:T(1024)S(1)}, f32[1024]{0:T(1024)}, u32[]{:S(2)}) copy-start(f32[1024]{0:T(1024)} %param.27) | copy-start | bytes 12292
  27.6 25.6 %copy-start.33 = (f32[1,16,256]{1,2,0:T(8,128)}, f32[1,16,256]{1,2,0:T(8,128)S(1)}, u32[]{:S(2)}) copy-start(f32[1,16,256]{1,2,0:T(8,128)S(1)} %get-tuple-element.387) | copy-start | bytes 49156
  27.6 25.6 %copy-start.29 = (f32[1,16,256]{1,2,0:T(8,128)}, f32[1,16,256]{1,2,0:T(8,128)S(1)}, u32[]{:S(2)}) copy-start(f32[1,16,256]{1,2,0:T(8,128)S(1)} %get-tuple-element.388) | copy-start | bytes 49156
  29.2 24.0 %copy-start.24 = (f32[1,16,256]{1,2,0:T(8,128)}, f32[1,16,256]{1,2,0:T(8,128)S(1)}, u32[]{:S(2)}) copy-start(f32[1,16,256]{1,2,0:T(8,128)S(1)} %get-tuple-element.372) | copy-start | bytes 49156
  53.2 18.5 %copy-start.21 = (f32[1,256,256]{2,1,0:T(8,128)}, f32[1,256,256]{2,1,0:T(8,128)S(1)}, u32[]{:S(2)}) copy-start(f32[1,256,256]{2,1,0:T(8,128)S(1)} %convolution_bitcast_fusion.3) | copy-start | bytes 786436
  53.2 15.8 %copy-start.65 = (f32[16]{0:T(128)}, f32[16]{0:T(128)S(1)}, u32[]{:S(2)}) copy-start(f32[16]{0:T(128)S(1)} %get-tuple-element.381) | copy-start | bytes 196
  69.0 2.6 collective-permute-start
  77.2 29.0 %copy-start.7 = (f32[1,256,1024]{1,2,0:T(8,128)}, f32[1,256,1024]{1,2,0:T(8,128)S(1)}, u32[]{:S(2)}) copy-start(f32[1,256,1024]{1,2,0:T(8,128)S(1)} %copy.193) | copy-start | bytes 3145732
  80.2 9.8 %copy-start.35 = (f32[256,16]{1,0:T(8,128)S(1)}, f32[256,16]{1,0:T(8,128)}, u32[]{:S(2)}) copy-start(f32[256,16]{1,0:T(8,128)} %get-tuple-element.371) | copy-start | bytes 49156
  80.2 71.5 %all-gather.15.cloned.1.call-start = ((), (), s32[]{:S(2)}) async-start(), calls=%async_computation.11 | async-start | bytes 2621440 | tf_op jit(solution)/shard_map/all_gather | solution.py:93
  80.9 117.2 %all-gather.17.cloned.1.call-start = ((), (), s32[]{:S(2)}) async-start(), calls=%async_computation.12 | async-start | bytes 2621440 | tf_op jit(solution)/shard_map/all_gather | solution.py:97
  81.5 162.7 %all-gather.27.cloned.1.call-start = ((), (), s32[]{:S(2)}) async-start(), calls=%async_computation.25 | async-start | bytes 2621440 | tf_op jit(solution)/shard_map/all_gather | solution.py:21
  104.2 8.1 %copy-start.73 = (f32[4,1,16]{2,1,0:T(1,128)}, f32[4,1,16]{2,1,0:T(1,128)S(1)}, u32[]{:S(2)}) copy-start(f32[4,1,16]{2,1,0:T(1,128)S(1)} %get-tuple-element.628) | copy-start | bytes 772
  114.9 83.3 %copy-start.45 = (f32[1024]{0:T(1024)S(1)}, f32[1024]{0:T(1024)}, u32[]{:S(2)}) copy-start(f32[1024]{0:T(1024)} %param.37) | copy-start | bytes 12292
  155.4 69.0 %copy-start.5 = (f32[256,1024]{1,0:T(8,128)}, f32[256,1024]{1,0:T(8,128)S(1)}, u32[]{:S(2)}) copy-start(f32[256,1024]{1,0:T(8,128)S(1)} %get-tuple-element.370) | copy-start | bytes 3145732
  218.4 99.9 %reduce-scatter.15.cloned.1.call-start = ((), (), s32[]{:S(2)}) async-start(), calls=%async_computation.13 | async-start | bytes 5242880 | tf_op jit(solution)/shard_map/reduce_scatter | solution.py:235
  224.3 173.7 %reduce-scatter.29.cloned.1.call-start = ((), (), s32[]{:S(2)}) async-start(), calls=%async_computation.22 | async-start | bytes 5242880 | tf_op jit(solution)/shard_map/reduce_scatter | solution.py:239
  228.3 249.3 %reduce-scatter.19.cloned.1.call-start = ((), (), s32[]{:S(2)}) async-start(), calls=%async_computation.16 | async-start | bytes 5242880 | tf_op jit(solution)/shard_map/reduce_scatter | solution.py:236
  231.0 10.1 %copy-start.13 = (f32[256,1024]{0,1:T(8,128)S(1)}, f32[256,1024]{0,1:T(8,128)}, u32[]{:S(2)}) copy-start(f32[256,1024]{0,1:T(8,128)} %copy.208) | copy-start | bytes 3145732
  281.0 3.1 collective-permute-start.1
  289.5 210.5 %reduce-scatter.27.cloned.1.call-start = ((), (), s32[]{:S(2)}) async-start(), calls=%async_computation.21 | async-start | bytes 81920 | tf_op jit(solution)/shard_map/reduce_scatter | solution.py:238
  293.1 7.2 copy-start.11
  299.3 15.4 %copy-start.40 = (bf16[1,16,256]{1,2,0:T(8,128)(2,1)}, bf16[1,16,256]{1,2,0:T(8,128)(2,1)S(1)}, u32[]{:S(2)}) copy-start(bf16[1,16,256]{1,2,0:T(8,128)(2,1)S(1)} %get-tuple-element.365) | copy-start | bytes 24580
  300.3 227.8 %reduce-scatter.23.cloned.1.call-start = ((), (), s32[]{:S(2)}) async-start(), calls=%async_computation.19 | async-start | bytes 1310720 | tf_op jit(solution)/shard_map/reduce_scatter | solution.py:237
  314.8 239.6 %reduce-scatter.17.cloned.1.call-start = ((), (), s32[]{:S(2)}) async-start(), calls=%async_computation.14 | async-start | bytes 1310720 | tf_op jit(solution)/shard_map/reduce_scatter | solution.py:242
  318.3 263.4 %reduce-scatter.33.cloned.1.call-start = ((), (), s32[]{:S(2)}) async-start(), calls=%async_computation.27 | async-start | bytes 1310720
  400.5 77.1 %copy-start.6 = (f32[256,1024]{1,0:T(8,128)S(1)}, f32[256,1024]{1,0:T(8,128)}, u32[]{:S(2)}) copy-start(f32[256,1024]{1,0:T(8,128)} %copy-done.5) | copy-start | bytes 3145732
  400.6 208.8 %reduce-scatter.21.cloned.1.call-start = ((), (), s32[]{:S(2)}) async-start(), calls=%async_computation.17 | async-start | bytes 1310720 | tf_op jit(solution)/shard_map/reduce_scatter | solution.py:243
  477.6 154.2 %reduce-scatter.31.cloned.1.call-start = ((), (), s32[]{:S(2)}) async-start(), calls=%async_computation.26 | async-start | bytes 163840
  482.7 18.8 %copy-start.41 = (bf16[1,16,256]{1,2,0:T(8,128)(2,1)S(1)}, bf16[1,16,256]{1,2,0:T(8,128)(2,1)}, u32[]{:S(2)}) copy-start(bf16[1,16,256]{1,2,0:T(8,128)(2,1)} %copy-done.40) | copy-start | bytes 24580
  482.8 18.8 %copy-start.43 = (bf16[1024,16]{0,1:T(8,128)(2,1)S(1)}, bf16[1024,16]{0,1:T(8,128)(2,1)}, u32[]{:S(2)}) copy-start(bf16[1024,16]{0,1:T(8,128)(2,1)} %copy-done.42) | copy-start | bytes 98308
  501.5 196.8 %all-reduce.11.cloned.1.call-start = ((), (), s32[]{:S(2)}) async-start(), calls=%async_computation.28 | async-start | bytes 4194304 | tf_op jit(solution)/shard_map/psum | solution.py:146
  502.8 106.5 %copy-start.56 = (f32[1024]{0:T(1024)S(1)}, f32[1024]{0:T(1024)}, u32[]{:S(2)}) copy-start(f32[1024]{0:T(1024)} %get-tuple-element.362) | copy-start | bytes 12292
  502.8 106.7 %copy-start.49 = (f32[1,1280]{1,0:T(1,128)S(1)}, f32[1,1280]{1,0:T(1,128)}, u32[]{:S(2)}) copy-start(f32[1,1280]{1,0:T(1,128)} %copy-done.48) | copy-start | bytes 15364
  502.8 106.7 %copy-start.51 = (f32[1,1280]{1,0:T(1,128)S(1)}, f32[1,1280]{1,0:T(1,128)}, u32[]{:S(2)}) copy-start(f32[1,1280]{1,0:T(1,128)} %copy-done.50) | copy-start | bytes 15364
  502.8 106.7 %copy-start.53 = (f32[1,1280]{1,0:T(1,128)S(1)}, f32[1,1280]{1,0:T(1,128)}, u32[]{:S(2)}) copy-start(f32[1,1280]{1,0:T(1,128)} %copy-done.52) | copy-start | bytes 15364
  502.9 106.7 %copy-start.55 = (f32[1,1280]{1,0:T(1,128)S(1)}, f32[1,1280]{1,0:T(1,128)}, u32[]{:S(2)}) copy-start(f32[1,1280]{1,0:T(1,128)} %copy-done.54) | copy-start | bytes 15364
  502.9 195.5 %copy-start.27 = (bf16[1024,256]{1,0:T(8,128)(2,1)S(1)}, bf16[1024,256]{1,0:T(8,128)(2,1)}, u32[]{:S(2)}) copy-start(bf16[1024,256]{1,0:T(8,128)(2,1)} %copy-done.26) | copy-start | bytes 1572868
  502.9 231.2 %reduce-scatter.25.cloned.1.call-start = ((), (), s32[]{:S(2)}) async-start(), calls=%async_computation.20 | async-start | bytes 327680 | tf_op jit(solution)/shard_map/reduce_scatter | solution.py:244
  528.2 212.0 %all-gather.19.cloned.1.call-start = ((), (), s32[]{:S(2)}) async-start(), calls=%async_computation.15 | async-start | bytes 1310720 | tf_op jit(solution)/shard_map/all_gather | solution.py:249
  554.4 204.3 %all-gather.23.cloned.1.call-start = ((), (), s32[]{:S(2)}) async-start(), calls=%async_computation.23 | async-start | bytes 1310720 | tf_op jit(solution)/shard_map/all_gather | solution.py:253
  581.7 195.3 %all-gather.21.cloned.1.call-start = ((), (), s32[]{:S(2)}) async-start(), calls=%async_computation.18 | async-start | bytes 1310720 | tf_op jit(solution)/shard_map/all_gather | solution.py:250
  698.4 33.0 %copy-start.28 = (bf16[1,256,1024]{2,1,0:T(8,128)(2,1)S(1)}, bf16[1,256,1024]{2,1,0:T(8,128)(2,1)}, u32[]{:S(2)}) copy-start(bf16[1,256,1024]{2,1,0:T(8,128)(2,1)} %param.39) | copy-start | bytes 1572868
  698.4 33.0 %copy-start.70 = (f32[256]{0:T(256)S(1)}, f32[256]{0:T(256)}, u32[]{:S(2)}) copy-start(f32[256]{0:T(256)} %get-tuple-element.383) | copy-start | bytes 3076
  740.1 36.9 %copy-start.31 = (f32[256,1024]{1,0:T(8,128)S(1)}, f32[256,1024]{1,0:T(8,128)}, u32[]{:S(2)}) copy-start(f32[256,1024]{1,0:T(8,128)} %all-gather.19.cloned.1.call-done) | copy-start | bytes 3145732
  (50 other events, 143.0 us)
Sparse Core Ops, SparseCore 0:
  9.6 56.9 all-gather.12
  80.3 23.7 all-gather.24
  105.7 45.9 all-gather.14
  153.1 45.0 all-gather.16
  218.5 20.8 all-gather.26
  241.5 76.7 reduce-scatter.14
  320.7 77.2 reduce-scatter.28
  400.3 77.2 reduce-scatter.18
  480.5 19.5 reduce-scatter.26
  502.7 25.3 reduce-scatter.22
  530.8 23.5 reduce-scatter.16
  556.8 24.8 reduce-scatter.32
  584.4 24.8 reduce-scatter.20
  612.2 19.5 reduce-scatter.30
  635.2 63.0 all-reduce.10
  700.7 20.0 reduce-scatter.24
  722.3 17.1 all-gather.18
  741.0 17.6 all-gather.22
  760.3 16.7 all-gather.20
